TPU v7x, 768 devices: a whole 4x8x12 slice. The times are simulated.
768 devices in a mesh: dp: 32 (over y, z_hi, core), mp: 6 (over z_lo), group: 4 (over x).
Axes of the slice: x: 4, y: 8, z: 12 (z_hi: 2, z_lo: 6; z = z_hi * 6 + z_lo), core: 2. Of those that a mesh axis runs over, the one named last changes fastest.
Arguments:
- frames: bfloat16 [55296, 1024], P(('dp', 'mp')), may hold values from -6 to 6
- frame_keep: int32 [55296], P(('dp', 'mp')), may hold values 0 or 1
- destination: int32 [13824, 1], P(('dp', 'mp')), may hold values from 0 to 31; in each aligned block of 72 rows (0 to 71, 72 to 143, ...) at most 3 rows name the same one
- ln_gain: float32 [1024], replicated, may hold values from 0.1 to 1.9
- ln_bias: float32 [1024], replicated, may hold values from -3 to 3
- w_in: bfloat16 [1024, 4096], P(None, 'group'), may hold values from -0.1875 to 0.1875
- w_out: bfloat16 [4096, 1024], P('group'), may hold values from -0.09375 to 0.09375
- upstream: bfloat16 [73728, 1024], P(('dp', 'mp')), may hold values from -6 to 6
Outputs:
- encoded: bfloat16 [73728, 1024], P(('dp', 'mp'))
- w_in_grad: float32 [1024, 4096], P('dp', 'group')
- w_out_grad: float32 [4096, 1024], P('group', 'dp')
Inputs may be any that keep to these rules, and one draw needn't show every extreme that they name: At most 3 blocks of one device have the same destination, and in every draw some device sends exactly 3 blocks to one destination.
All inputs are finite; a program needn't handle non-finite values. No bound on the sum of `frame_keep` on one device may be relied on, other than what follows from the above.
Results may differ from a plain program's by a relative error of at most 0.024.
Values may be sent and summed in bfloat16 or wider, within the bound.
A program may use at most 64 MiB of HBM per device.

v0:
```python
import jax
import jax.numpy as jnp
from jax import lax
from jax.sharding import PartitionSpec as P


def shards(frames, frame_keep, destination, ln_gain, ln_bias, w_in, w_out, upstream):
    row_count, feat_width = frames.shape
    peer_count = lax.axis_size("dp")
    block_count = destination.shape[0]
    frame_run = row_count // block_count
    slot_count = upstream.shape[0] // frame_run
    capacity = slot_count // peer_count
    target = destination[:, 0]
    chosen = (target[:, None] == jnp.arange(peer_count, dtype=jnp.int32)[None, :]).astype(jnp.int32)
    before = jnp.cumsum(chosen, axis=0) - chosen
    rank_in = jnp.sum(before * chosen, axis=1)
    slot_of = target * capacity + rank_in
    placing = (slot_of[None, :] == jnp.arange(slot_count, dtype=jnp.int32)[:, None]).astype(
        jnp.bfloat16
    )
    block_frames = frames.reshape(block_count, frame_run * feat_width)
    packed = jnp.dot(placing, block_frames, preferred_element_type=jnp.float32).astype(jnp.bfloat16)
    keep_blocks = frame_keep.astype(jnp.bfloat16).reshape(block_count, frame_run)
    packed_keep = jnp.dot(placing, keep_blocks, preferred_element_type=jnp.float32).astype(
        jnp.bfloat16
    )
    packed = packed.reshape(peer_count, capacity * frame_run, feat_width)
    packed_keep = packed_keep.reshape(peer_count, capacity * frame_run)
    arrived, arrived_keep = (
        lax.all_to_all(packed, "dp", split_axis=0, concat_axis=0, tiled=True),
        lax.all_to_all(packed_keep, "dp", split_axis=0, concat_axis=0, tiled=True),
    )
    incoming = arrived.reshape(-1, feat_width)
    live_rows = arrived_keep.reshape(-1, 1).astype(jnp.float32)
    features = incoming.astype(jnp.float32)
    row_mean = jnp.mean(features, axis=1, keepdims=True)
    centered = features - row_mean
    row_var = jnp.mean(centered * centered, axis=1, keepdims=True)
    normed = (centered * lax.rsqrt(row_var + 1e-05) * ln_gain + ln_bias).astype(jnp.bfloat16)
    preact = jnp.dot(normed, w_in, preferred_element_type=jnp.float32)
    hidden = (preact * jax.nn.sigmoid(preact)).astype(jnp.bfloat16)
    partial_value = jnp.dot(hidden, w_out, preferred_element_type=jnp.float32)
    total = lax.psum(partial_value.astype(jnp.bfloat16), "group").astype(jnp.float32)
    encoded = (live_rows * (features + 0.5 * total)).astype(jnp.bfloat16)
    grad_scale = float(row_count * peer_count * lax.axis_size("mp")) ** (-0.5)
    row_grad = (0.5 * grad_scale * live_rows * upstream.astype(jnp.float32)).astype(jnp.bfloat16)
    contract_rows = (((0,), (0,)), ((), ()))
    out_term = lax.dot_general(row_grad, hidden, contract_rows, preferred_element_type=jnp.float32)
    back_hidden = lax.dot_general(
        row_grad, w_out, (((1,), (1,)), ((), ())), preferred_element_type=jnp.float32
    )
    sigmoid_pre = jax.nn.sigmoid(preact)
    act_grad = (back_hidden * (sigmoid_pre + preact * sigmoid_pre * (1.0 - sigmoid_pre))).astype(
        jnp.bfloat16
    )
    in_term = lax.dot_general(normed, act_grad, contract_rows, preferred_element_type=jnp.float32)
    both_rows = lax.psum_scatter(
        jnp.stack([in_term, out_term]).astype(jnp.bfloat16), "dp", scatter_dimension=1, tiled=True
    ).astype(jnp.float32)
    in_rows_sum = both_rows[0]
    out_rows_sum = both_rows[1]
    in_final, out_final = (
        lax.psum(in_rows_sum.astype(jnp.bfloat16), "mp").astype(jnp.float32),
        lax.psum(out_rows_sum.astype(jnp.bfloat16), "mp").astype(jnp.float32),
    )
    return (encoded, in_final, out_final.T)


def solution(mesh):
    placed = (
        P(("dp", "mp"), None),
        P(("dp", "mp")),
        P(("dp", "mp"), None),
        P(),
        P(),
        P(None, "group"),
        P("group", None),
        P(("dp", "mp"), None),
    )
    return jax.shard_map(
        shards,
        mesh=mesh,
        in_specs=placed,
        out_specs=(P(("dp", "mp"), None), P("dp", "group"), P("group", "dp")),
        check_vma=False,
    )
```

profile of v0, /device:TPU:1, one launch (start us, length us, event | category | flops | bytes accessed | tf_op | source)
XLA Modules:
  0.0 381.2 jit_solution(8616047557944395644)
XLA Ops:
  8.0 0.0 copy-start
  8.0 0.8 convert_element_type.76
  8.8 0.1 reshape.83
  9.0 0.7 fusion.3
  9.7 0.1 reduce_window_sum.11
  9.8 0.8 select_reduce_fusion
  10.7 0.7 multiply_add_fusion
  11.3 0.2 convolution_convert_fusion.2
  11.5 0.1 copy.12
  11.6 0.7 all_to_all.12
  12.3 21.4 %all-to-all-start = ((bf16[32,1,12]{2,1,0:T(2,128)(2,1)}), bf16[32,1,12]{2,1,0:T(2,128)(2,1)S(1)}, u32[]{:S(2)}, u32[]{:S(2)}) async-start(bf16[32,1,12]{2,1,0:T(2,128)(2,1)} %all_to_all.12), calls=%async_computation | async-start | bytes 32768 | tf_op jit(solution)/shard_map/all_to_all | solution.py:32
  33.8 1.5 reshape.84
  35.2 0.4 convolution_convert_fusion
  35.6 1.7 reshape.85
  37.3 10.5 %all-to-all-done = bf16[32,1,12]{2,1,0:T(2,128)(2,1)S(1)} async-done(((bf16[32,1,12]{2,1,0:T(2,128)(2,1)}), bf16[32,1,12]{2,1,0:T(2,128)(2,1)S(1)}, u32[]{:S(2)}, u32[]{:S(2)}) %all-to-all-start) | async-done | bytes 800 | tf_op jit(solution)/shard_map/all_to_all | solution.py:32
  47.8 4.2 %all-to-all-start.1 = ((bf16[32,12,1024]{2,1,0:T(8,128)(2,1)}), bf16[32,12,1024]{2,1,0:T(8,128)(2,1)S(1)}, u32[]{:S(2)}, u32[]{:S(2)}) async-start(bf16[32,12,1024]{2,1,0:T(8,128)(2,1)} %reshape.85), calls=%async_computation.1 | async-start | bytes 2097152 | tf_op jit(solution)/shard_map/all_to_all | solution.py:31
  52.1 0.0 reduce-scatter.2.cloned.1.call-start
  52.1 0.1 convert_reduce_fusion.1
  52.2 0.1 reshape.86
  52.3 28.2 %all-to-all-done.1 = bf16[32,12,1024]{2,1,0:T(8,128)(2,1)S(1)} async-done(((bf16[32,12,1024]{2,1,0:T(8,128)(2,1)}), bf16[32,12,1024]{2,1,0:T(8,128)(2,1)S(1)}, u32[]{:S(2)}, u32[]{:S(2)}) %all-to-all-start.1) | async-done | bytes 786464 | tf_op jit(solution)/shard_map/all_to_all | solution.py:31
  80.5 0.2 convert_reduce_fusion
  80.8 0.1 div.13
  80.9 0.4 multiply_reduce_fusion
  81.3 0.0 copy-start.2
  81.3 0.0 copy-start.3
  81.3 0.1 rsqrt.12
  81.4 1.4 reshape.87
  82.8 0.0 copy-done.2
  82.8 0.0 copy-done.3
  82.8 3.2 fusion.7
  86.0 1.1 copy-done.4
  87.2 0.0 copy-done.1
  87.2 2.8 convert_bitcast_fusion
  90.0 5.6 %convert_bitcast_fusion.1 = bf16[1,1024,1024]{2,1,0:T(8,128)(2,1)} fusion(bf16[1024,1024]{1,0:T(8,128)(2,1)S(1)} %copy-done, f32[384,1024]{1,0:T(8,128)} %copy-done.4, bf16[384,1024]{1,0:T(8,128)(2,1)S(1)} %copy-done.1, f32[384]{0:T(512)S(1)} %broadcast_multiply_fusion.1, f32[384,1024]{1,0:T(8,128)} %reshape.87, f32[1024]{0:T(1024)S(1)} %copy-done.2, ...), kind=kOutput, calls=%fused_computation.3 | convolution fusion | flops 1618345984 | bytes 8139264 | tf_op jit(solution)/shard_map/dot_general | solution.py:57
  95.6 4.5 %pad_maximum_fusion = bf16[2,1024,1024]{2,1,0:T(8,128)(2,1)} fusion(bf16[1,1024,1024]{2,1,0:T(8,128)(2,1)} %convert_bitcast_fusion, bf16[1,1024,1024]{2,1,0:T(8,128)(2,1)} %convert_bitcast_fusion.1), kind=kLoop, calls=%fused_computation.1 | loop fusion | flops 2097152 | bytes 8388608 | tf_op jit(solution)/shard_map/stack | solution.py:59
  100.1 0.0 reduce-scatter.2.cloned.1.call-update
  100.1 0.0 all-reduce.4.cloned.1.call-start
  100.2 3.3 convolution_convert_fusion.1
  103.5 0.0 all-reduce.4.cloned.1.call-update
  103.5 0.0 all-reduce.6.cloned.1.call-start
  103.6 181.9 %reduce-scatter.2.cloned.1.call-done = bf16[2,32,1024]{2,1,0:T(8,128)(2,1)} async-done(((bf16[2,1024,1024]{2,1,0:T(8,128)(2,1)}), bf16[2,32,1024]{2,1,0:T(8,128)(2,1)}) %reduce-scatter.2.cloned.1.call-update) | async-done | bytes 131088 | tf_op jit(solution)/shard_map/reduce_scatter | solution.py:58
  285.5 1.5 slice_bitcast_fusion
  287.0 0.0 all-reduce.6.cloned.1.call-update
  287.0 0.0 all-reduce.4.cloned.1.call-done
  287.1 2.7 multiply_convert_fusion.2
  289.8 81.0 %all-reduce.6.cloned.1.call-done = (bf16[32,1024]{1,0:T(8,128)(2,1)}, bf16[1024,32]{0,1:T(8,128)(2,1)}) async-done(((bf16[32,1024]{1,0:T(8,128)(2,1)}, bf16[1024,32]{0,1:T(8,128)(2,1)}), (bf16[32,1024]{1,0:T(8,128)(2,1)}, bf16[1024,32]{0,1:T(8,128)(2,1)})) %all-reduce.6.cloned.1.call-update) | async-done | bytes 131088 | tf_op jit(solution)/shard_map/psum | solution.py:64
  370.8 1.5 convert_element_type.93
  372.3 1.5 transpose.17
  (6 shorter events, 0.0 us)
Async XLA Ops:
  8.0 82.0 %copy-start = (bf16[1024,1024]{1,0:T(8,128)(2,1)S(1)}, bf16[1024,1024]{1,0:T(8,128)(2,1)}, u32[]{:S(2)}) copy-start(bf16[1024,1024]{1,0:T(8,128)(2,1)} %param.14) | copy-start | bytes 6291460
  12.3 35.5 %all-to-all-start = ((bf16[32,1,12]{2,1,0:T(2,128)(2,1)}), bf16[32,1,12]{2,1,0:T(2,128)(2,1)S(1)}, u32[]{:S(2)}, u32[]{:S(2)}) async-start(bf16[32,1,12]{2,1,0:T(2,128)(2,1)} %all_to_all.12), calls=%async_computation | async-start | bytes 32768 | tf_op jit(solution)/shard_map/all_to_all | solution.py:32
  47.8 32.7 %all-to-all-start.1 = ((bf16[32,12,1024]{2,1,0:T(8,128)(2,1)}), bf16[32,12,1024]{2,1,0:T(8,128)(2,1)S(1)}, u32[]{:S(2)}, u32[]{:S(2)}) async-start(bf16[32,12,1024]{2,1,0:T(8,128)(2,1)} %reshape.85), calls=%async_computation.1 | async-start | bytes 2097152 | tf_op jit(solution)/shard_map/all_to_all | solution.py:31
  52.1 233.4 %reduce-scatter.2.cloned.1.call-start = ((), (), s32[]{:S(2)}) async-start(), calls=%async_computation.4 | async-start | bytes 4325376 | tf_op jit(solution)/shard_map/reduce_scatter | solution.py:58
  81.3 1.5 copy-start.2
  81.3 1.5 copy-start.3
  82.8 4.3 %copy-start.1 = (bf16[384,1024]{1,0:T(8,128)(2,1)S(1)}, bf16[384,1024]{1,0:T(8,128)(2,1)}, u32[]{:S(2)}) copy-start(bf16[384,1024]{1,0:T(8,128)(2,1)} %param.15) | copy-start | bytes 2359300
  86.0 1.1 copy-start.4
  100.1 186.9 %all-reduce.4.cloned.1.call-start = ((), (), s32[]{:S(2)}) async-start(), calls=%async_computation.3 | async-start | bytes 1572864 | tf_op jit(solution)/shard_map/psum | solution.py:44
  103.5 267.3 %all-reduce.6.cloned.1.call-start = ((), (), s32[]{:S(2)}) async-start(), calls=%async_computation.5 | async-start | bytes 262144 | tf_op jit(solution)/shard_map/psum | solution.py:64
Sparse Core Ops, SparseCore 0:
  100.3 185.1 reduce-scatter.1
Sparse Core Ops, SparseCore 1:
  103.6 73.3 all-reduce.3
  287.1 83.6 all-reduce.5
where the time goes:
time: 385 us; the launch traced here: 381 us
  waiting for transfers between devices  302 us (78%)
  starting transfers between devices  25.8 us (7%)
  between operations  15.6 us (4%)
  matrix products  15.4 us (4%)
  other arithmetic  14.2 us (4%)
  local copies, waits for them, and re-layouts  8.51 us (2%)
    reduce_scatter x1, waiting for transfers between devices, shards(): lax.psum_scatter(jnp.stack([in_term, out_term]).astype(jnp.bfloat16), 'dp...  182 us
    psum x1, waiting for transfers between devices, shards(): lax.psum(in_rows_sum.astype(jnp.bfloat16), 'mp').astype(jnp.float32)  81 us
    all_to_all x1, waiting for transfers between devices, shards(): lax.all_to_all(packed, 'dp', split_axis=0, concat_axis=0, tiled=True)  28.2 us
    all_to_all x1, starting transfers between devices, shards(): lax.all_to_all(packed_keep, 'dp', split_axis=0, concat_axis=0, tiled=True)  21.4 us
    all_to_all x1, waiting for transfers between devices, shards(): lax.all_to_all(packed_keep, 'dp', split_axis=0, concat_axis=0, tiled=True)  10.5 us
  transfers between devices with their start and end apart: 5, of which 4 were waited for; matrix products, arithmetic and copies ran while one was open for 3% of the time, Pallas kernels for 0%

commit v1 on v0

v1 whole, which is shorter than its diff:
```python
import functools
import jax
import jax.numpy as jnp
from jax import lax
from jax.experimental import pallas as pl
from jax.experimental.pallas import tpu as pltpu
from jax.sharding import PartitionSpec as P

MESH = pl.DeviceIdType.MESH
NX = 4
NC = 2
NZH = 2
LANE = 128
ROWS16 = 16
F32 = jnp.float32
BF16 = jnp.bfloat16
I32 = jnp.int32


def iota(shape, axis):
    return lax.broadcasted_iota(I32, shape, axis)


def dot(a, b):
    return jnp.dot(a, b, preferred_element_type=F32)


def kernel(
    dims,
    dest_ref,
    keep_ref,
    frames_ref,
    gain_ref,
    bias_ref,
    w_in_hbm,
    w_out_hbm,
    up_ref,
    enc_ref,
    gin_ref,
    gout_ref,
    w_in,
    w_out,
    msg,
    arr,
    tok,
    ups,
    ups_t,
    back,
    nrm_t,
    hid,
    act,
    g_out,
    g_in,
    r_out,
    r_in,
    s_out,
    s_in,
    l_z,
    l_y,
    fin,
    asm,
    swp,
    p_own,
    p_oth,
    p_rcv,
    q_sum,
    q_rcv,
    w_sem,
    a_snd,
    a_rcv,
    u_snd,
    u_rcv,
    t_snd,
    t_rcv,
    o_snd,
    o_rcv,
    i_snd,
    i_rcv,
    z_snd,
    z_rcv,
    y_snd,
    y_rcv,
    f_snd,
    f_rcv,
    c_snd,
    c_rcv,
    p_snd,
    p_rsm,
    q_snd,
    q_rsm,
    e_snd,
    e_rcv,
):
    ny, nzl, cap, run, scale = dims
    nz = NZH * nzl
    rows, width = up_ref.shape
    half = w_in.shape[1]
    slab = rows // ny
    pair_rows = cap * run
    panels = half // LANE
    own_rows = width // (ny * NZH)
    prow = panels * own_rows
    piece = fin.shape[2]
    quarter = rows // NX
    ygroup = ny // NX

    dp = lax.axis_index("dp")
    y = lax.div(dp, 4)
    zh = lax.rem(lax.div(dp, 2), 2)
    c = lax.rem(dp, 2)
    zl = lax.axis_index("mp")
    x = lax.axis_index("group")
    z = zh * nzl + zl
    pc = 1 - c

    def wrap(v, n):
        return lax.rem(v + n, n)

    def at_y(v):
        return {"dp": v * 4 + zh * 2 + c}

    def at_z(v):
        return {"dp": y * 4 + lax.div(v, nzl) * 2 + c, "mp": lax.rem(v, nzl)}

    def at_x(v):
        return {"group": v}

    partner = {"dp": y * 4 + zh * 2 + pc}

    started = []

    def send(src, dst, snd, rcv, where):
        copy = pltpu.make_async_remote_copy(
            src_ref=src, dst_ref=dst, send_sem=snd, recv_sem=rcv, device_id=where, device_id_type=MESH
        )
        copy.start()
        started.append(copy)
        return copy

    get_w_in = pltpu.make_async_copy(w_in_hbm.at[:, pl.ds(pl.multiple_of(c * half, half), half)], w_in, w_sem.at[0])
    get_w_out = pltpu.make_async_copy(w_out_hbm.at[pl.ds(pl.multiple_of(c * half, half), half), :], w_out, w_sem.at[1])
    get_w_out.start()
    get_w_in.start()

    barrier = pltpu.get_barrier_semaphore()
    greeted = 0
    kinds = [(g, dz, dc) for g in range(ygroup) for dz in range(2) for dc in range(2)]

    def a2a_id(yy, dz, dc):
        zz = (1 - zh) if dz else zh
        cc = pc if dc else c
        return {"dp": yy * 4 + zz * 2 + cc}

    sources = []
    for g, dz, dc in kinds:
        if dz or dc:
            sources.append(a2a_id(wrap(y - x - NX * g + ny, ny), dz, dc))
    sources += [at_y(wrap(y - d, ny)) for d in range(1, ny)]
    sources += [at_z(wrap(z - d, nz)) for d in range(1, nz)]
    sources += [at_x(wrap(x - d, NX)) for d in range(1, NX)]
    sources += [partner]
    for where in sources:
        pl.semaphore_signal(barrier, inc=1, device_id=where, device_id_type=MESH)

    nb = dest_ref.shape[1]
    nf = nb * run
    bi, bj = iota((nb, nb), 0), iota((nb, nb), 1)
    drow = jnp.broadcast_to(dest_ref[...], (nb, nb))
    dcol = jnp.sum(jnp.where(bi == bj, drow, 0), axis=1, keepdims=True)
    rank = jnp.sum(jnp.where((dcol == drow) & (bi < bj), 1, 0), axis=0, keepdims=True)
    slot = (dest_ref[...] * cap + rank).astype(F32).astype(BF16)
    spread = (iota((nb, nf), 0) == lax.div(iota((nb, nf), 1), run)).astype(F32).astype(BF16)
    slot_f = dot(jnp.broadcast_to(slot, (8, nb)), spread)[0:1, :]
    nm = len(kinds)
    mi = iota((nm * ROWS16, 1), 0)
    mk, mr = lax.div(mi, ROWS16), lax.rem(mi, ROWS16)
    mg, mdz, mdc = lax.div(mk, 4), lax.rem(lax.div(mk, 2), 2), lax.rem(mk, 2)
    my = lax.rem(y + x + NX * mg, ny)
    mzh = lax.rem(zh + mdz, 2)
    mc = lax.rem(c + mdc, 2)
    want = ((my * 4 + mzh * 2 + mc) * cap + lax.div(mr, run)).astype(F32)
    shape = (nm * ROWS16, nf)
    hit = (
        (jnp.broadcast_to(slot_f, shape) == jnp.broadcast_to(want, shape))
        & (lax.rem(iota(shape, 1), run) == jnp.broadcast_to(lax.rem(mr, run), shape))
        & (jnp.broadcast_to(mr, shape) < pair_rows)
    )
    place = jnp.where(hit, 1.0, 0.0)
    msg[:, :width] = dot(place.astype(BF16), frames_ref[...]).astype(BF16)
    keep_row = keep_ref[...].astype(F32)
    keep_col = jnp.sum(place * keep_row, axis=1, keepdims=True)
    msg[:, width:] = jnp.broadcast_to(keep_col, (nm * ROWS16, LANE)).astype(BF16)
    mine = pl.ds(pl.multiple_of(c * rows, rows), rows)
    theirs = pl.ds(pl.multiple_of(pc * rows, rows), rows)
    ups[mine, :] = (scale * up_ref[...].astype(F32)).astype(BF16)

    pl.semaphore_wait(barrier, len(sources))

    a2a = []
    for k, (g, dz, dc) in enumerate(kinds):
        spot = pl.ds(pl.multiple_of((g * 4 + zh * 2 + c) * ROWS16, ROWS16), ROWS16)
        part = msg.at[pl.ds(k * ROWS16, ROWS16), :]
        copy = pltpu.make_async_remote_copy(
            src_ref=part,
            dst_ref=arr.at[spot, :],
            send_sem=a_snd.at[k],
            recv_sem=a_rcv.at[k],
            device_id=a2a_id(lax.rem(y + x + NX * g, ny), dz, dc),
            device_id_type=MESH,
        )
        if k == 0:
            local = pltpu.make_async_copy(part, arr.at[spot, :], a_rcv.at[k])

            @pl.when(x == 0)
            def _(local=local):
                local.start()

            @pl.when(x != 0)
            def _(copy=copy):
                copy.start()
        else:
            copy.start()
        a2a.append(copy)
    ucopy = send(ups.at[mine, :], ups.at[mine, :], u_snd.at[0], u_rcv.at[0], partner)

    get_w_out.wait()
    for where in (mine, theirs):
        if where is theirs:
            ucopy.wait_recv()
        u = ups[where, :]
        back[where, :] = lax.dot_general(u, w_out[...], (((1,), (1,)), ((), ())), preferred_element_type=F32)
        ups_t[:, where] = u.T
    get_w_in.wait()

    for k in range(nm):
        if k == 0:

            @pl.when(x == 0)
            def _():
                local.wait()

            @pl.when(x != 0)
            def _():
                a2a[0].wait()
        else:
            a2a[k].wait()

    cq = ygroup * slab
    ci, cj = iota((cq, nm * ROWS16), 0), iota((cq, nm * ROWS16), 1)
    squeeze = (cj == lax.div(ci, pair_rows) * ROWS16 + lax.rem(ci, pair_rows)).astype(F32).astype(BF16)
    compact = dot(squeeze, arr[...]).astype(BF16)

    def rows_of(origin, g):
        ys = lax.rem(y - origin - NX * g + 2 * ny, ny)
        return tok.at[pl.ds(pl.multiple_of(c * rows + ys * slab, ROWS16), slab), :]

    def t_at(second, o, g):
        return second * 8 + o * 2 + g

    xn, xp, xo = wrap(x + 1, NX), wrap(x - 1, NX), wrap(x + 2, NX)
    origins = {0: x, 1: xn, 2: xo, 3: xp}

    def t_send(o, g, second, slot_at_receiver, tag, where):
        ref = rows_of(origins[o], g)
        return send(ref, ref, t_snd.at[tag], t_rcv.at[t_at(second, slot_at_receiver, g)], where)

    waits = {}
    for g in range(ygroup):
        rows_of(x, g)[...] = compact[g * slab : (g + 1) * slab, :]
        waits[3, g] = t_send(0, g, 0, 3, g, at_x(xn))
        waits[1, g] = t_send(0, g, 0, 1, 2 + g, at_x(xp))
        waits["c", 0, g] = t_send(0, g, 1, 0, 4 + g, partner)
    waits[3, 0].wait_recv()
    waits[2, 0] = t_send(3, 0, 0, 2, 6, at_x(xn))
    waits["c", 3, 0] = t_send(3, 0, 1, 3, 8, partner)
    waits[1, 1].wait_recv()
    waits[2, 1] = t_send(1, 1, 0, 2, 7, at_x(xp))
    waits["c", 1, 1] = t_send(1, 1, 1, 1, 9, partner)
    waits[3, 1].wait_recv()
    waits["c", 3, 1] = t_send(3, 1, 1, 3, 10, partner)
    waits[1, 0].wait_recv()
    waits["c", 1, 0] = t_send(1, 0, 1, 1, 11, partner)
    for g in range(ygroup):
        waits[2, g].wait_recv()
        waits["c", 2, g] = t_send(2, g, 1, 2, 12 + g, partner)
    for o in range(NX):
        for g in range(ygroup):
            waits["c", o, g].wait_recv()

    step_rows = LANE
    for t in range(2 * rows // step_rows):
        at = pl.ds(t * step_rows, step_rows)
        feat = tok[at, :width].astype(F32)
        live = tok[at, width:][:, 0:1].astype(F32)
        mean = jnp.mean(feat, axis=1, keepdims=True)
        cen = feat - mean
        var = jnp.mean(cen * cen, axis=1, keepdims=True)
        norm = (cen * lax.rsqrt(var + 1e-05) * gain_ref[...] + bias_ref[...]).astype(BF16)
        nrm_t[:, at] = norm.T
        pre = dot(norm, w_in[...])
        sig = jax.nn.sigmoid(pre)
        hid[at, :] = (live * (pre * sig)).astype(BF16)
        act[at, :] = (live * back[at, :] * (sig + pre * sig * (1.0 - sig))).astype(BF16)

    def gradient(left, right, out):
        block = 2 * LANE
        for b in range(width // block):
            val = dot(left[pl.ds(b * block, block), :], right[...]).astype(BF16)
            for u in range(block // own_rows):
                unit = b * (block // own_rows) + u
                for p in range(panels):
                    out[unit % NZH, unit // NZH, pl.ds(p * own_rows, own_rows), :] = val[
                        u * own_rows : (u + 1) * own_rows, p * LANE : (p + 1) * LANE
                    ]

    def start_of(j):
        return pl.multiple_of(jnp.minimum(j * piece, prow - piece), ROWS16)

    ysteps = ny // 2
    ochain = {}

    def o_step(s):
        for d in range(2):
            sign = 1 - 2 * d
            for h in range(2):
                first = 1 if d == h else 2
                if s < first:
                    continue
                target = wrap(y + sign * (ysteps + 1 - s), ny)
                if s == first:
                    src = g_out.at[h, target]
                else:
                    ochain[d, h, s - 1].wait_recv()
                    src = r_out.at[d, h, s - 2]
                    src[...] = (src[...].astype(F32) + g_out[h, target].astype(F32)).astype(BF16)
                tag = (d * 2 + h) * ysteps + s - 1
                ochain[d, h, s] = send(
                    src, r_out.at[d, h, s - 1], o_snd.at[tag], o_rcv.at[tag], at_y(wrap(y + sign, ny))
                )

    zsteps = nz // 2
    ichain = {}
    hy = ny // 2

    def i_own(h, v):
        return g_in.at[lax.div(v, nzl), pl.ds(h * hy, hy), pl.ds(start_of(lax.rem(v, nzl)), piece), :]

    def i_step(s):
        for d in range(2):
            sign = 1 - 2 * d
            for h in range(2):
                first = 1 if d == h else 2
                if s < first:
                    continue
                own = i_own(h, wrap(z + sign * (zsteps + 1 - s), nz))
                if s == first:
                    src = own
                else:
                    ichain[d, h, s - 1].wait_recv()
                    src = r_in.at[d, h, s - 2]
                    src[...] = (src[...].astype(F32) + own[...].astype(F32)).astype(BF16)
                tag = (d * 2 + h) * zsteps + s - 1
                ichain[d, h, s] = send(
                    src, r_in.at[d, h, s - 1], i_snd.at[tag], i_rcv.at[tag], at_z(wrap(z + sign, nz))
                )

    gradient(ups_t, hid, g_out)
    o_step(1)
    gradient(nrm_t, act, g_in)
    i_step(1)
    p_oth[...] = dot(hid[theirs, :], w_out[...]).astype(BF16)
    pcopy = send(p_oth, p_rcv, p_snd.at[0], p_rsm.at[0], partner)
    o_step(2)
    i_step(2)
    p_own[...] = dot(hid[mine, :], w_out[...])
    o_step(3)
    pcopy.wait_recv()
    q_sum[...] = (p_own[...] + p_rcv[...].astype(F32)).astype(BF16)
    qcopies = []
    for d in range(1, NX):
        to = wrap(x + d, NX)
        part = q_sum.at[pl.ds(pl.multiple_of(to * quarter, quarter), quarter), :]
        qcopies.append(send(part, q_rcv.at[d - 1], q_snd.at[d - 1], q_rsm.at[d - 1], at_x(to)))
    i_step(3)
    o_step(4)
    i_step(4)

    zcopies = []
    for h in range(2):
        ochain[0, h, ysteps].wait_recv()
        ochain[1, h, ysteps].wait_recv()
        s_out[h] = (
            g_out[h, y].astype(F32)
            + r_out[0, h, ysteps - 1].astype(F32)
            + r_out[1, h, ysteps - 1].astype(F32)
        ).astype(BF16)
    for d in range(1, nz):
        to = wrap(z + d, nz)
        part = s_out.at[lax.div(to, nzl), pl.ds(start_of(lax.rem(to, nzl)), piece), :]
        zcopies.append(send(part, l_z.at[d - 1], z_snd.at[d - 1], z_rcv.at[d - 1], at_z(to)))
    i_step(5)

    for q in qcopies:
        q.wait_recv()
    xrows = pl.ds(pl.multiple_of(x * quarter, quarter), quarter)
    total = q_sum[xrows, :].astype(F32)
    for d in range(1, NX):
        total = total + q_rcv[d - 1].astype(F32)
    trows = pl.ds(pl.multiple_of(c * rows + x * quarter, ROWS16), quarter)
    feat = tok[trows, :width].astype(F32)
    live = tok[trows, width:][:, 0:1].astype(F32)
    enc_ref[xrows, :] = (live * (feat + 0.5 * total)).astype(BF16)
    ecopies = []
    for d in range(1, NX):
        part = enc_ref.at[xrows, :]
        ecopies.append(send(part, part, e_snd.at[d - 1], e_rcv.at[d - 1], at_x(wrap(x + d, NX))))
    i_step(6)

    for h in range(2):
        ichain[0, h, zsteps].wait_recv()
        ichain[1, h, zsteps].wait_recv()
        s_in[pl.ds(h * hy, hy)] = (
            i_own(h, z)[...].astype(F32)
            + r_in[0, h, zsteps - 1].astype(F32)
            + r_in[1, h, zsteps - 1].astype(F32)
        ).astype(BF16)
    ycopies = []
    for d in range(1, ny):
        to = wrap(y + d, ny)
        ycopies.append(send(s_in.at[to], l_y.at[d - 1], y_snd.at[d - 1], y_rcv.at[d - 1], at_y(to)))

    for q in zcopies:
        q.wait_recv()
    sum_out = s_out[zh, pl.ds(start_of(zl), piece), :].astype(F32)
    for d in range(1, nz):
        sum_out = sum_out + l_z[d - 1].astype(F32)
    fin[1, zl] = sum_out.astype(BF16)
    for q in ycopies:
        q.wait_recv()
    sum_in = s_in[y].astype(F32)
    for d in range(1, ny):
        sum_in = sum_in + l_y[d - 1].astype(F32)
    fin[0, zl] = sum_in.astype(BF16)

    fcopies = []
    for d in range(1, nzl):
        to = wrap(zl + d, nzl)
        part = fin.at[:, zl]
        fcopies.append(send(part, part, f_snd.at[d - 1], f_rcv.at[d - 1], {"dp": dp, "mp": to}))
    for q in fcopies:
        q.wait_recv()
    for u in range(prow // ROWS16):
        row = u * ROWS16
        j = next(j for j in range(nzl) if min(j * piece, prow - piece) <= row < min(j * piece, prow - piece) + piece)
        off = row - min(j * piece, prow - piece)
        for t in range(2):
            asm[t, row // own_rows, pl.ds(row % own_rows, ROWS16), :] = fin[t, j, pl.ds(off, ROWS16), :]
    core_rows = own_rows // NC
    ccopy = send(
        asm.at[:, :, pl.ds(pl.multiple_of(pc * core_rows, core_rows), core_rows), :],
        swp,
        c_snd.at[0],
        c_rcv.at[0],
        partner,
    )
    ccopy.wait_recv()
    for t, ref in enumerate((gin_ref, gout_ref)):
        for p in range(panels):
            own = asm[t, p, pl.ds(pl.multiple_of(c * core_rows, core_rows), core_rows), :].astype(F32)
            other = swp[t, p].astype(F32)
            ref[:, pl.ds(pl.multiple_of(c * half + p * LANE, LANE), LANE)] = own
            ref[:, pl.ds(pl.multiple_of(pc * half + p * LANE, LANE), LANE)] = other

    for q in ecopies:
        q.wait_recv()
    for q in started:
        q.wait_send()


def shards(ny, nzl, frames, frame_keep, destination, ln_gain, ln_bias, w_in, w_out, upstream):
    nf, width = frames.shape
    nb = destination.shape[0]
    run = nf // nb
    rows = upstream.shape[0]
    cap = rows // (run * ny * 4)
    units = w_in.shape[1]
    half = units // NC
    own_rows = width // (ny * NZH)
    panels = half // LANE
    prow = panels * own_rows
    piece = -(-prow // (nzl * ROWS16)) * ROWS16
    nz = NZH * nzl
    ygroup = ny // NX
    nm = ygroup * 4
    grad_scale = float(nf * ny * 4 * nzl) ** (-0.5)
    quarter = rows // NX
    ysteps, zsteps = ny // 2, nz // 2
    core_rows = own_rows // NC
    dma = pltpu.SemaphoreType.DMA
    vm = pltpu.VMEM
    pairs = [2, nm, 1, 16, 4 * ysteps, 4 * zsteps, nz - 1, ny - 1, nzl - 1, 1, 1, NX - 1, NX - 1]
    sems = []
    for i, n in enumerate(pairs):
        sems += [dma((n,))] if i == 0 else [dma((n,)), dma((n,))]
    vspec = pl.BlockSpec(memory_space=pltpu.VMEM)
    aspec = pl.BlockSpec(memory_space=pl.ANY)
    enc, gin, gout = pl.pallas_call(
        functools.partial(kernel, (ny, nzl, cap, run, 0.5 * grad_scale)),
        out_shape=(
            jax.ShapeDtypeStruct((rows, width), BF16),
            jax.ShapeDtypeStruct((core_rows, units), F32),
            jax.ShapeDtypeStruct((core_rows, units), F32),
        ),
        in_specs=[vspec, vspec, vspec, vspec, vspec, aspec, aspec, vspec],
        out_specs=(vspec, vspec, vspec),
        scratch_shapes=[
            vm((width, half), BF16),
            vm((half, width), BF16),
            vm((nm * ROWS16, width + LANE), BF16),
            vm((nm * ROWS16, width + LANE), BF16),
            vm((NC * rows, width + LANE), BF16),
            vm((NC * rows, width), BF16),
            vm((width, NC * rows), BF16),
            vm((NC * rows, half), F32),
            vm((width, NC * rows), BF16),
            vm((NC * rows, half), BF16),
            vm((NC * rows, half), BF16),
            vm((NZH, ny, prow, LANE), BF16),
            vm((NZH, ny, prow, LANE), BF16),
            vm((2, 2, ysteps, prow, LANE), BF16),
            vm((2, 2, zsteps, ny // 2, piece, LANE), BF16),
            vm((NZH, prow, LANE), BF16),
            vm((ny, piece, LANE), BF16),
            vm((nz - 1, piece, LANE), BF16),
            vm((ny - 1, piece, LANE), BF16),
            vm((2, nzl, piece, LANE), BF16),
            vm((2, panels, own_rows, LANE), BF16),
            vm((2, panels, core_rows, LANE), BF16),
            vm((rows, width), F32),
            vm((rows, width), BF16),
            vm((rows, width), BF16),
            vm((rows, width), BF16),
            vm((NX - 1, quarter, width), BF16),
        ]
        + sems,
        compiler_params=pltpu.CompilerParams(
            collective_id=0, has_side_effects=True, vmem_limit_bytes=56 * 1024 * 1024
        ),
        name="ffn_step",
    )(
        destination.reshape(1, nb),
        frame_keep.reshape(1, nf),
        frames,
        ln_gain.reshape(1, width),
        ln_bias.reshape(1, width),
        w_in,
        w_out,
        upstream,
    )
    return (enc, gin, gout.T)


def solution(mesh):
    placed = (
        P(("dp", "mp"), None),
        P(("dp", "mp")),
        P(("dp", "mp"), None),
        P(),
        P(),
        P(None, "group"),
        P("group", None),
        P(("dp", "mp"), None),
    )
    ny = mesh.shape["dp"] // (NZH * NC)
    return jax.shard_map(
        functools.partial(shards, ny, mesh.shape["mp"]),
        mesh=mesh,
        in_specs=placed,
        out_specs=(P(("dp", "mp"), None), P("dp", "group"), P("group", "dp")),
        check_vma=False,
    )
```

time: 385 us -> 101 us (0.26); the launches traced: 381 us -> 101 us
  waiting for transfers between devices: 302 us -> 0 us
  Pallas kernels: 0 us -> 94.1 us
  starting transfers between devices: 25.8 us -> 0 us
  matrix products: 15.4 us -> 0 us
  between operations: 15.6 us -> 0.64 us
  other arithmetic: 14.2 us -> 0 us
    reduce_scatter x1 -> x0, waiting for transfers between devices: 182 us -> none  [shards(): lax.psum_scatter(jnp.stack([in_term, out_term]).astype(jnp.bfloat16), 'dp...]
    pallas_call x0 -> x1, Pallas kernels: none -> 94.1 us  [shards(): pl.pallas_call(functools.partial(kernel, (ny, nzl, cap, run, 0.5 * grad_s...]
    psum x2 -> x0, waiting for transfers between devices: 81 us -> none  [the longest x1 81 us: shards(): lax.psum(in_rows_sum.astype(jnp.bfloat16), 'mp').astype(jnp.float32)]
    all_to_all x2 -> x0, waiting for transfers between devices: 38.7 us -> none  [the longest x1 28.2 us: shards(): lax.all_to_all(packed, 'dp', split_axis=0, concat_axis=0, tiled=True)]
    all_to_all x2 -> x0, starting transfers between devices: 25.7 us -> none  [the longest x1 21.4 us: shards(): lax.all_to_all(packed_keep, 'dp', split_axis=0, concat_axis=0, tiled=True)]
    dot_general x6 -> x0, matrix products: 15.4 us -> none  [the longest x1 5.59 us: shards(): lax.dot_general(normed, act_grad, contract_rows, preferred_element_type=j...]
    convert_element_type x5 -> x0, other arithmetic: 5.84 us -> none  [the longest x1 2.72 us: shards(): encoded = (live_rows * (features + 0.5 * total)).astype(jnp.bfloat16)]
    another operation x2 -> x0, other arithmetic: 4.64 us -> none  [the longest x1 4.53 us: shards(): jnp.stack([in_term, out_term]).astype(jnp.bfloat16)]
  transfers between devices with their start and end apart: 5 -> 0, of which waited for: 4 -> 0; matrix products, arithmetic and copies ran while one was open for 3% -> 0% of each run, Pallas kernels for 0% -> 0%
where the time goes in v1:
time: 101 us
  Pallas kernels  94.1 us (93%)
  local copies, waits for them, and re-layouts  6.44 us (6%)
    pallas_call x1, Pallas kernels, shards(): pl.pallas_call(functools.partial(kernel, (ny, nzl, cap, run, 0.5 * grad_s...  94.1 us
    unnamed x3, local copies, waits for them, and re-layouts  5.2 us

profile of v1, /device:TPU:1, one launch (start us, length us, event | category | flops | bytes accessed | tf_op | source)
XLA Modules:
  0.0 101.2 jit_solution(17449691378470104733)
XLA Ops:
  0.6 1.2 %reshape.19.keep_ref = s32[1,288]{1,0:T(1,128)} reshape(s32[288]{0:T(512)} %param.9) | data formatting | bytes 2304 | tf_op jit(solution)/shard_map/reshape | solution.py:552
  1.9 94.1 %ffn_step.1 = (bf16[384,1024]{1,0:T(8,128)(2,1)}, f32[32,1024]{1,0:T(8,128)}, f32[32,1024]{1,0:T(8,128)}) custom-call(s32[1,72]{1,0:T(1,128)} %bitcast.7, s32[1,288]{1,0:T(1,128)} %reshape.19.keep_ref, bf16[288,1024]{1,0:T(8,128)(2,1)} %frames_ref.1, f32[1,1024]{1,0:T(1,128)} %bitcast.5, f32[1,1024]{1,0:T(1,128)} %bitcast.6, bf16[1024,1024]{1,0:T(8,128)(2,1)} %w_in_hbm.1, ...), custom_call_target="tpu_custom_call" | custom-call | tf_op jit(solution)/shard_map/ffn_step/pallas_call | solution.py:507
  96.0 2.1 %copy.14 = bf16[384,1024]{1,0:T(8,128)(2,1)} copy(bf16[384,1024]{1,0:T(8,128)(2,1)} %get-tuple-element.12) | data formatting | bytes 1572864
  98.1 1.6 %copy.15 = f32[32,1024]{1,0:T(8,128)} copy(f32[32,1024]{1,0:T(8,128)} %get-tuple-element.13) | data formatting | bytes 262144
  99.6 1.6 %copy.16 = f32[1024,32]{0,1:T(8,128)} copy(f32[1024,32]{0,1:T(8,128)} %bitcast.4) | data formatting | bytes 262144

commit v2 on v1

--- a/solution.py
+++ b/solution.py
@@ -15,6 +15,8 @@
 F32 = jnp.float32
 BF16 = jnp.bfloat16
 I32 = jnp.int32
+OPARTS = 2
+IPARTS = 2
 
 
 def iota(shape, axis):
@@ -57,9 +59,8 @@
     s_in,
     l_z,
     l_y,
+    pce,
     fin,
-    asm,
-    swp,
     p_own,
     p_oth,
     p_rcv,
@@ -82,8 +83,6 @@
     y_rcv,
     f_snd,
     f_rcv,
-    c_snd,
-    c_rcv,
     p_snd,
     p_rsm,
     q_snd,
@@ -100,7 +99,10 @@
     panels = half // LANE
     own_rows = width // (ny * NZH)
     prow = panels * own_rows
-    piece = fin.shape[2]
+    core_rows = own_rows // NC
+    core_span = panels * core_rows
+    per_core = nzl // NC
+    piece = pce.shape[1]
     quarter = rows // NX
     ygroup = ny // NX
 
@@ -158,6 +160,7 @@
     sources += [at_y(wrap(y - d, ny)) for d in range(1, ny)]
     sources += [at_z(wrap(z - d, nz)) for d in range(1, nz)]
     sources += [at_x(wrap(x - d, NX)) for d in range(1, NX)]
+    sources += [{"dp": y * 4 + zh * 2 + pc, "mp": wrap(zl - d, nzl)} for d in range(1, nzl)]
     sources += [partner]
     for where in sources:
         pl.semaphore_signal(barrier, inc=1, device_id=where, device_id_type=MESH)
@@ -187,17 +190,18 @@
     )
     place = jnp.where(hit, 1.0, 0.0)
     msg[:, :width] = dot(place.astype(BF16), frames_ref[...]).astype(BF16)
-    keep_row = keep_ref[...].astype(F32)
+    keep_row = keep_ref[...].reshape(1, nf).astype(F32)
     keep_col = jnp.sum(place * keep_row, axis=1, keepdims=True)
     msg[:, width:] = jnp.broadcast_to(keep_col, (nm * ROWS16, LANE)).astype(BF16)
     mine = pl.ds(pl.multiple_of(c * rows, rows), rows)
     theirs = pl.ds(pl.multiple_of(pc * rows, rows), rows)
-    ups[mine, :] = (scale * up_ref[...].astype(F32)).astype(BF16)
 
     pl.semaphore_wait(barrier, len(sources))
 
     a2a = []
-    for k, (g, dz, dc) in enumerate(kinds):
+
+    def a2a_send(k):
+        g, dz, dc = kinds[k]
         spot = pl.ds(pl.multiple_of((g * 4 + zh * 2 + c) * ROWS16, ROWS16), ROWS16)
         part = msg.at[pl.ds(k * ROWS16, ROWS16), :]
         copy = pltpu.make_async_remote_copy(
@@ -208,47 +212,52 @@
             device_id=a2a_id(lax.rem(y + x + NX * g, ny), dz, dc),
             device_id_type=MESH,
         )
-        if k == 0:
-            local = pltpu.make_async_copy(part, arr.at[spot, :], a_rcv.at[k])
-
-            @pl.when(x == 0)
-            def _(local=local):
-                local.start()
-
-            @pl.when(x != 0)
-            def _(copy=copy):
-                copy.start()
-        else:
+        a2a.append(copy)
+        if k:
             copy.start()
-        a2a.append(copy)
-    ucopy = send(ups.at[mine, :], ups.at[mine, :], u_snd.at[0], u_rcv.at[0], partner)
-
-    get_w_out.wait()
-    for where in (mine, theirs):
-        if where is theirs:
-            ucopy.wait_recv()
+            return None
+        local = pltpu.make_async_copy(part, arr.at[spot, :], a_rcv.at[k])
+
+        @pl.when(x == 0)
+        def _():
+            local.start()
+
+        @pl.when(x != 0)
+        def _():
+            copy.start()
+
+        return local
+
+    def back_of(where):
         u = ups[where, :]
         back[where, :] = lax.dot_general(u, w_out[...], (((1,), (1,)), ((), ())), preferred_element_type=F32)
         ups_t[:, where] = u.T
-    get_w_in.wait()
-
-    for k in range(nm):
-        if k == 0:
-
-            @pl.when(x == 0)
-            def _():
-                local.wait()
+
+    locals_of = {}
+    for k in range(4):
+        locals_of[k] = a2a_send(k)
+    local = locals_of[0]
+    ups[mine, :] = (scale * up_ref[...].astype(F32)).astype(BF16)
+    ucopy = send(ups.at[mine, :], ups.at[mine, :], u_snd.at[0], u_rcv.at[0], partner)
+    get_w_out.wait()
+    back_of(mine)
+    for k in range(4):
+        if k:
+            a2a[k].wait_send()
+        else:
 
             @pl.when(x != 0)
             def _():
-                a2a[0].wait()
-        else:
-            a2a[k].wait()
-
-    cq = ygroup * slab
-    ci, cj = iota((cq, nm * ROWS16), 0), iota((cq, nm * ROWS16), 1)
+                a2a[0].wait_send()
+
+    for k in range(4, nm):
+        a2a_send(k)
+    ucopy.wait_recv()
+    back_of(theirs)
+    get_w_in.wait()
+
+    ci, cj = iota((slab, 4 * ROWS16), 0), iota((slab, 4 * ROWS16), 1)
     squeeze = (cj == lax.div(ci, pair_rows) * ROWS16 + lax.rem(ci, pair_rows)).astype(F32).astype(BF16)
-    compact = dot(squeeze, arr[...]).astype(BF16)
 
     def rows_of(origin, g):
         ys = lax.rem(y - origin - NX * g + 2 * ny, ny)
@@ -266,9 +275,27 @@
 
     waits = {}
     for g in range(ygroup):
-        rows_of(x, g)[...] = compact[g * slab : (g + 1) * slab, :]
-        waits[3, g] = t_send(0, g, 0, 3, g, at_x(xn))
-        waits[1, g] = t_send(0, g, 0, 1, 2 + g, at_x(xp))
+        for k in range(g * 4, g * 4 + 4):
+            if k == 0:
+
+                @pl.when(x == 0)
+                def _():
+                    local.wait()
+
+                @pl.when(x != 0)
+                def _():
+                    a2a[0].wait_recv()
+            elif k < 4:
+                a2a[k].wait_recv()
+            else:
+                a2a[k].wait()
+        rows_of(x, g)[...] = dot(squeeze, arr[pl.ds(g * 4 * ROWS16, 4 * ROWS16), :]).astype(BF16)
+        if g == 0:
+            waits[3, g] = t_send(0, g, 0, 3, g, at_x(xn))
+            waits[1, g] = t_send(0, g, 0, 1, 2 + g, at_x(xp))
+        else:
+            waits[1, g] = t_send(0, g, 0, 1, 2 + g, at_x(xp))
+            waits[3, g] = t_send(0, g, 0, 3, g, at_x(xn))
         waits["c", 0, g] = t_send(0, g, 1, 0, 4 + g, partner)
     waits[3, 0].wait_recv()
     waits[2, 0] = t_send(3, 0, 0, 2, 6, at_x(xn))
@@ -276,14 +303,14 @@
     waits[1, 1].wait_recv()
     waits[2, 1] = t_send(1, 1, 0, 2, 7, at_x(xp))
     waits["c", 1, 1] = t_send(1, 1, 1, 1, 9, partner)
+    waits[1, 0].wait_recv()
+    waits["c", 1, 0] = t_send(1, 0, 1, 1, 11, partner)
     waits[3, 1].wait_recv()
     waits["c", 3, 1] = t_send(3, 1, 1, 3, 10, partner)
-    waits[1, 0].wait_recv()
-    waits["c", 1, 0] = t_send(1, 0, 1, 1, 11, partner)
     for g in range(ygroup):
         waits[2, g].wait_recv()
         waits["c", 2, g] = t_send(2, g, 1, 2, 12 + g, partner)
-    for o in range(NX):
+    for o in (0, 3, 1, 2):
         for g in range(ygroup):
             waits["c", o, g].wait_recv()
 
@@ -308,72 +335,88 @@
             val = dot(left[pl.ds(b * block, block), :], right[...]).astype(BF16)
             for u in range(block // own_rows):
                 unit = b * (block // own_rows) + u
-                for p in range(panels):
-                    out[unit % NZH, unit // NZH, pl.ds(p * own_rows, own_rows), :] = val[
-                        u * own_rows : (u + 1) * own_rows, p * LANE : (p + 1) * LANE
-                    ]
+                for e in range(NC):
+                    for p in range(panels):
+                        row = u * own_rows + e * core_rows
+                        out[unit % NZH, unit // NZH, pl.ds((e * panels + p) * core_rows, core_rows), :] = val[
+                            row : row + core_rows, p * LANE : (p + 1) * LANE
+                        ]
 
     def start_of(j):
-        return pl.multiple_of(jnp.minimum(j * piece, prow - piece), ROWS16)
+        core_at = lax.div(j, per_core)
+        inside = jnp.minimum(lax.rem(j, per_core) * piece, core_span - piece)
+        return pl.multiple_of(core_at * core_span + inside, ROWS16)
 
     ysteps = ny // 2
     ochain = {}
-
-    def o_step(s):
+    ocut = OPARTS // NZH
+    orows = prow // ocut
+
+    def o_own(q, v):
+        return g_out.at[q // ocut, v, pl.ds(q % ocut * orows, orows), :]
+
+    def o_step(phase, s):
         for d in range(2):
             sign = 1 - 2 * d
-            for h in range(2):
-                first = 1 if d == h else 2
-                if s < first:
+            for q in range(OPARTS):
+                if (d == q % 2) != (phase == 0):
                     continue
-                target = wrap(y + sign * (ysteps + 1 - s), ny)
-                if s == first:
-                    src = g_out.at[h, target]
-                else:
-                    ochain[d, h, s - 1].wait_recv()
-                    src = r_out.at[d, h, s - 2]
-                    src[...] = (src[...].astype(F32) + g_out[h, target].astype(F32)).astype(BF16)
-                tag = (d * 2 + h) * ysteps + s - 1
-                ochain[d, h, s] = send(
-                    src, r_out.at[d, h, s - 1], o_snd.at[tag], o_rcv.at[tag], at_y(wrap(y + sign, ny))
-                )
-
-    zsteps = nz // 2
-    ichain = {}
-    hy = ny // 2
-
-    def i_own(h, v):
-        return g_in.at[lax.div(v, nzl), pl.ds(h * hy, hy), pl.ds(start_of(lax.rem(v, nzl)), piece), :]
-
-    def i_step(s):
-        for d in range(2):
-            sign = 1 - 2 * d
-            for h in range(2):
-                first = 1 if d == h else 2
-                if s < first:
-                    continue
-                own = i_own(h, wrap(z + sign * (zsteps + 1 - s), nz))
+                first = 1 + phase
+                own = o_own(q, wrap(y + sign * (ysteps + 1 - s), ny))
                 if s == first:
                     src = own
                 else:
-                    ichain[d, h, s - 1].wait_recv()
-                    src = r_in.at[d, h, s - 2]
+                    ochain[d, q, s - 1].wait_recv()
+                    src = r_out.at[d, q, s - 2]
                     src[...] = (src[...].astype(F32) + own[...].astype(F32)).astype(BF16)
-                tag = (d * 2 + h) * zsteps + s - 1
-                ichain[d, h, s] = send(
-                    src, r_in.at[d, h, s - 1], i_snd.at[tag], i_rcv.at[tag], at_z(wrap(z + sign, nz))
+                tag = (d * OPARTS + q) * ysteps + s - 1
+                ochain[d, q, s] = send(
+                    src, r_out.at[d, q, s - 1], o_snd.at[tag], o_rcv.at[tag], at_y(wrap(y + sign, ny))
                 )
 
+    zsteps = nz // 2
+    ichain = {}
+    hy = ny // IPARTS
+
+    def i_own(q, v):
+        return g_in.at[lax.div(v, nzl), pl.ds(q * hy, hy), pl.ds(start_of(lax.rem(v, nzl)), piece), :]
+
+    def i_step(phase, s):
+        for d in range(2):
+            sign = 1 - 2 * d
+            for q in range(IPARTS):
+                if (d == q % 2) != (phase == 0):
+                    continue
+                first = 1 + phase
+                own = i_own(q, wrap(z + sign * (zsteps + 1 - s), nz))
+                if s == first:
+                    src = own
+                else:
+                    ichain[d, q, s - 1].wait_recv()
+                    src = r_in.at[d, q, s - 2]
+                    src[...] = (src[...].astype(F32) + own[...].astype(F32)).astype(BF16)
+                tag = (d * IPARTS + q) * zsteps + s - 1
+                ichain[d, q, s] = send(
+                    src, r_in.at[d, q, s - 1], i_snd.at[tag], i_rcv.at[tag], at_z(wrap(z + sign, nz))
+                )
+
+    gradient(nrm_t, act, g_in)
+    i_step(0, 1)
     gradient(ups_t, hid, g_out)
-    o_step(1)
-    gradient(nrm_t, act, g_in)
-    i_step(1)
+    o_step(0, 1)
+    i_step(1, 2)
     p_oth[...] = dot(hid[theirs, :], w_out[...]).astype(BF16)
+    o_step(1, 2)
     pcopy = send(p_oth, p_rcv, p_snd.at[0], p_rsm.at[0], partner)
-    o_step(2)
-    i_step(2)
+    i_step(0, 2)
+    o_step(0, 2)
     p_own[...] = dot(hid[mine, :], w_out[...])
-    o_step(3)
+    i_step(1, 3)
+    o_step(1, 3)
+    i_step(0, 3)
+    o_step(0, 3)
+    i_step(1, 4)
+    o_step(1, 4)
     pcopy.wait_recv()
     q_sum[...] = (p_own[...] + p_rcv[...].astype(F32)).astype(BF16)
     qcopies = []
@@ -381,25 +424,79 @@
         to = wrap(x + d, NX)
         part = q_sum.at[pl.ds(pl.multiple_of(to * quarter, quarter), quarter), :]
         qcopies.append(send(part, q_rcv.at[d - 1], q_snd.at[d - 1], q_rsm.at[d - 1], at_x(to)))
-    i_step(3)
-    o_step(4)
-    i_step(4)
+    i_step(0, 4)
+    o_step(0, 4)
+    i_step(1, 5)
+    i_step(0, 5)
 
     zcopies = []
-    for h in range(2):
-        ochain[0, h, ysteps].wait_recv()
-        ochain[1, h, ysteps].wait_recv()
-        s_out[h] = (
-            g_out[h, y].astype(F32)
-            + r_out[0, h, ysteps - 1].astype(F32)
-            + r_out[1, h, ysteps - 1].astype(F32)
+    for q in range(OPARTS):
+        ochain[0, q, ysteps].wait_recv()
+        ochain[1, q, ysteps].wait_recv()
+        s_out[q // ocut, pl.ds(q % ocut * orows, orows), :] = (
+            o_own(q, y)[...].astype(F32)
+            + r_out[0, q, ysteps - 1].astype(F32)
+            + r_out[1, q, ysteps - 1].astype(F32)
         ).astype(BF16)
     for d in range(1, nz):
         to = wrap(z + d, nz)
         part = s_out.at[lax.div(to, nzl), pl.ds(start_of(lax.rem(to, nzl)), piece), :]
         zcopies.append(send(part, l_z.at[d - 1], z_snd.at[d - 1], z_rcv.at[d - 1], at_z(to)))
-    i_step(5)
-
+    i_step(1, 6)
+    i_step(0, 6)
+
+    for q in range(IPARTS):
+        ichain[0, q, zsteps].wait_recv()
+        ichain[1, q, zsteps].wait_recv()
+        s_in[pl.ds(q * hy, hy)] = (
+            i_own(q, z)[...].astype(F32)
+            + r_in[0, q, zsteps - 1].astype(F32)
+            + r_in[1, q, zsteps - 1].astype(F32)
+        ).astype(BF16)
+    ycopies = []
+    for d in range(1, ny):
+        to = wrap(y + d, ny)
+        ycopies.append(send(s_in.at[to], l_y.at[d - 1], y_snd.at[d - 1], y_rcv.at[d - 1], at_y(to)))
+
+    home = lax.div(zl, per_core)
+    spot = c * per_core + lax.rem(zl, per_core)
+
+    def gather(t):
+        def base(d):
+            return pltpu.make_async_remote_copy(
+                src_ref=pce.at[t],
+                dst_ref=fin.at[t, spot],
+                send_sem=f_snd.at[t, d],
+                recv_sem=f_rcv.at[t, spot],
+                device_id={"dp": y * 4 + zh * 2 + home, "mp": wrap(zl + d, nzl)},
+                device_id_type=MESH,
+            )
+
+        @pl.when(home == c)
+        def _():
+            pltpu.make_async_copy(pce.at[t], fin.at[t, spot], f_rcv.at[t, spot]).start()
+
+        @pl.when(home != c)
+        def _():
+            base(0).start()
+
+        for d in range(1, nzl):
+            copy = base(d)
+            copy.start()
+            started.append(copy)
+        return base(0)
+
+    def gathered(t):
+        for slot in range(NC * per_core):
+            pltpu.make_async_copy(pce.at[t], fin.at[t, slot], f_rcv.at[t, slot]).wait()
+
+    for q in zcopies:
+        q.wait_recv()
+    sum_out = s_out[zh, pl.ds(start_of(zl), piece), :].astype(F32)
+    for d in range(1, nz):
+        sum_out = sum_out + l_z[d - 1].astype(F32)
+    pce[1] = sum_out.astype(BF16)
+    own_out = gather(1)
     for q in qcopies:
         q.wait_recv()
     xrows = pl.ds(pl.multiple_of(x * quarter, quarter), quarter)
@@ -414,67 +511,46 @@
     for d in range(1, NX):
         part = enc_ref.at[xrows, :]
         ecopies.append(send(part, part, e_snd.at[d - 1], e_rcv.at[d - 1], at_x(wrap(x + d, NX))))
-    i_step(6)
-
-    for h in range(2):
-        ichain[0, h, zsteps].wait_recv()
-        ichain[1, h, zsteps].wait_recv()
-        s_in[pl.ds(h * hy, hy)] = (
-            i_own(h, z)[...].astype(F32)
-            + r_in[0, h, zsteps - 1].astype(F32)
-            + r_in[1, h, zsteps - 1].astype(F32)
-        ).astype(BF16)
-    ycopies = []
-    for d in range(1, ny):
-        to = wrap(y + d, ny)
-        ycopies.append(send(s_in.at[to], l_y.at[d - 1], y_snd.at[d - 1], y_rcv.at[d - 1], at_y(to)))
-
-    for q in zcopies:
-        q.wait_recv()
-    sum_out = s_out[zh, pl.ds(start_of(zl), piece), :].astype(F32)
-    for d in range(1, nz):
-        sum_out = sum_out + l_z[d - 1].astype(F32)
-    fin[1, zl] = sum_out.astype(BF16)
+
     for q in ycopies:
         q.wait_recv()
     sum_in = s_in[y].astype(F32)
     for d in range(1, ny):
         sum_in = sum_in + l_y[d - 1].astype(F32)
-    fin[0, zl] = sum_in.astype(BF16)
-
-    fcopies = []
-    for d in range(1, nzl):
-        to = wrap(zl + d, nzl)
-        part = fin.at[:, zl]
-        fcopies.append(send(part, part, f_snd.at[d - 1], f_rcv.at[d - 1], {"dp": dp, "mp": to}))
-    for q in fcopies:
-        q.wait_recv()
-    for u in range(prow // ROWS16):
-        row = u * ROWS16
-        j = next(j for j in range(nzl) if min(j * piece, prow - piece) <= row < min(j * piece, prow - piece) + piece)
-        off = row - min(j * piece, prow - piece)
-        for t in range(2):
-            asm[t, row // own_rows, pl.ds(row % own_rows, ROWS16), :] = fin[t, j, pl.ds(off, ROWS16), :]
-    core_rows = own_rows // NC
-    ccopy = send(
-        asm.at[:, :, pl.ds(pl.multiple_of(pc * core_rows, core_rows), core_rows), :],
-        swp,
-        c_snd.at[0],
-        c_rcv.at[0],
-        partner,
-    )
-    ccopy.wait_recv()
-    for t, ref in enumerate((gin_ref, gout_ref)):
-        for p in range(panels):
-            own = asm[t, p, pl.ds(pl.multiple_of(c * core_rows, core_rows), core_rows), :].astype(F32)
-            other = swp[t, p].astype(F32)
-            ref[:, pl.ds(pl.multiple_of(c * half + p * LANE, LANE), LANE)] = own
-            ref[:, pl.ds(pl.multiple_of(pc * half + p * LANE, LANE), LANE)] = other
+    pce[0] = sum_in.astype(BF16)
+    own_in = gather(0)
+    gathered(1)
+    gathered(0)
+
+    @pl.when(home != c)
+    def _():
+        own_in.wait_send()
+        own_out.wait_send()
+
+    for e in range(NC):
+        for u in range(core_span // ROWS16):
+            row = u * ROWS16
+            j = next(j for j in range(per_core) if row < min(j * piece, core_span - piece) + piece)
+            off = row - min(j * piece, core_span - piece)
+            p, r = row // core_rows, row % core_rows
+            for t, ref in enumerate((gin_ref, gout_ref)):
+                ref[pl.ds(r, ROWS16), pl.ds(e * half + p * LANE, LANE)] = fin[
+                    t, e * per_core + j, pl.ds(off, ROWS16), :
+                ].astype(F32)
 
     for q in ecopies:
         q.wait_recv()
     for q in started:
         q.wait_send()
+
+
+def place_outputs(enc, gin, gout, enc_to, gin_to, gout_to, sem):
+    copies = []
+    for i, (src, dst) in enumerate(((enc, enc_to), (gin, gin_to), (gout, gout_to))):
+        copies.append(pltpu.make_async_copy(src, dst, sem.at[i]))
+        copies[i].start()
+    for copy in copies:
+        copy.wait()
 
 
 def shards(ny, nzl, frames, frame_keep, destination, ln_gain, ln_bias, w_in, w_out, upstream):
@@ -489,6 +565,7 @@
     panels = half // LANE
     prow = panels * own_rows
     piece = -(-prow // (nzl * ROWS16)) * ROWS16
+    per_core = nzl // NC
     nz = NZH * nzl
     ygroup = ny // NX
     nm = ygroup * 4
@@ -498,10 +575,11 @@
     core_rows = own_rows // NC
     dma = pltpu.SemaphoreType.DMA
     vm = pltpu.VMEM
-    pairs = [2, nm, 1, 16, 4 * ysteps, 4 * zsteps, nz - 1, ny - 1, nzl - 1, 1, 1, NX - 1, NX - 1]
+    pairs = [2, nm, 1, 16, 2 * OPARTS * ysteps, 2 * IPARTS * zsteps, nz - 1, ny - 1, (2, nzl), 1, NX - 1, NX - 1]
     sems = []
     for i, n in enumerate(pairs):
-        sems += [dma((n,))] if i == 0 else [dma((n,)), dma((n,))]
+        shape = n if isinstance(n, tuple) else (n,)
+        sems += [dma(shape)] if i == 0 else [dma(shape), dma(shape)]
     vspec = pl.BlockSpec(memory_space=pltpu.VMEM)
     aspec = pl.BlockSpec(memory_space=pl.ANY)
     enc, gin, gout = pl.pallas_call(
@@ -527,15 +605,14 @@
             vm((NC * rows, half), BF16),
             vm((NZH, ny, prow, LANE), BF16),
             vm((NZH, ny, prow, LANE), BF16),
-            vm((2, 2, ysteps, prow, LANE), BF16),
-            vm((2, 2, zsteps, ny // 2, piece, LANE), BF16),
+            vm((2, OPARTS, ysteps, prow * NZH // OPARTS, LANE), BF16),
+            vm((2, IPARTS, zsteps, ny // IPARTS, piece, LANE), BF16),
             vm((NZH, prow, LANE), BF16),
             vm((ny, piece, LANE), BF16),
             vm((nz - 1, piece, LANE), BF16),
             vm((ny - 1, piece, LANE), BF16),
-            vm((2, nzl, piece, LANE), BF16),
-            vm((2, panels, own_rows, LANE), BF16),
-            vm((2, panels, core_rows, LANE), BF16),
+            vm((2, piece, LANE), BF16),
+            vm((2, NC * per_core, piece, LANE), BF16),
             vm((rows, width), F32),
             vm((rows, width), BF16),
             vm((rows, width), BF16),
@@ -549,7 +626,7 @@
         name="ffn_step",
     )(
         destination.reshape(1, nb),
-        frame_keep.reshape(1, nf),
+        frame_keep,
         frames,
         ln_gain.reshape(1, width),
         ln_bias.reshape(1, width),
@@ -557,6 +634,14 @@
         w_out,
         upstream,
     )
+    enc, gin, gout = pl.pallas_call(
+        place_outputs,
+        out_shape=tuple(jax.ShapeDtypeStruct(v.shape, v.dtype) for v in (enc, gin, gout)),
+        in_specs=[vspec] * 3,
+        out_specs=(aspec,) * 3,
+        scratch_shapes=[dma((3,))],
+        name="place_outputs",
+    )(enc, gin, gout)
     return (enc, gin, gout.T)
 
 

time: 101 us -> 93.2 us (0.923)
  local copies, waits for them, and re-layouts: 6.44 us -> 0 us
  Pallas kernels: 94.1 us -> 92.4 us
    unnamed x3 -> x0, local copies, waits for them, and re-layouts: 5.2 us -> none
    pallas_call x1, Pallas kernels: 94.1 us -> 90.2 us  [shards(): pl.pallas_call(functools.partial(kernel, (ny, nzl, cap, run, 0.5 * grad_s...]
    pallas_call x0 -> x1, Pallas kernels: none -> 2.2 us  [shards(): pl.pallas_call(place_outputs, out_shape=tuple((jax.ShapeDtypeStruct(v.sha...]
    reshape x1 -> x0, local copies, waits for them, and re-layouts: 1.25 us -> none  [shards(): frame_keep.reshape(1, nf)]
where the time goes in v2:
time: 93.2 us; the launch traced here: 93 us
  Pallas kernels  92.4 us (99%)
    pallas_call x1, Pallas kernels, shards(): pl.pallas_call(functools.partial(kernel, (ny, nzl, cap, run, 0.5 * grad_s...  90.2 us
    pallas_call x1, Pallas kernels, shards(): pl.pallas_call(place_outputs, out_shape=tuple((jax.ShapeDtypeStruct(v.sha...  2.2 us

profile of v2, /device:TPU:1, one launch (start us, length us, event | category | flops | bytes accessed | tf_op | source)
XLA Modules:
  0.0 93.0 jit_solution(13432911432510316929)
XLA Ops:
  0.6 90.2 %ffn_step.1 = (bf16[384,1024]{1,0:T(8,128)(2,1)}, f32[32,1024]{1,0:T(8,128)}, f32[32,1024]{1,0:T(8,128)}) custom-call(s32[1,72]{1,0:T(1,128)} %bitcast.6, s32[288]{0:T(512)} %keep_ref.1, bf16[288,1024]{1,0:T(8,128)(2,1)} %frames_ref.1, f32[1,1024]{1,0:T(1,128)} %bitcast.4, f32[1,1024]{1,0:T(1,128)} %bitcast.5, bf16[1024,1024]{1,0:T(8,128)(2,1)} %w_in_hbm.1, ...), custom_call_target="tpu_custom_call" | custom-call | tf_op jit(solution)/shard_map/ffn_step/pallas_call | solution.py:585
  90.9 2.2 %place_outputs.1 = (bf16[384,1024]{1,0:T(8,128)(2,1)}, f32[32,1024]{1,0:T(8,128)}, f32[32,1024]{1,0:T(8,128)}) custom-call(bf16[384,1024]{1,0:T(8,128)(2,1)} %get-tuple-element.9.enc, f32[32,1024]{1,0:T(8,128)} %get-tuple-element.10.gin, f32[32,1024]{1,0:T(8,128)} %get-tuple-element.11.gout), custom_call_target="tpu_custom_call" | custom-call | tf_op jit(solution)/shard_map/place_outputs/pallas_call | solution.py:637

commit v3 on v2

--- a/solution.py
+++ b/solution.py
@@ -31,17 +31,19 @@
     dims,
     dest_ref,
     keep_ref,
-    frames_ref,
+    frames_hbm,
     gain_ref,
     bias_ref,
     w_in_hbm,
     w_out_hbm,
-    up_ref,
+    up_hbm,
     enc_ref,
     gin_ref,
     gout_ref,
     w_in,
     w_out,
+    frames_ref,
+    up_ref,
     msg,
     arr,
     tok,
@@ -105,6 +107,7 @@
     piece = pce.shape[1]
     quarter = rows // NX
     ygroup = ny // NX
+    mrows = msg.shape[0] // (ygroup * 4)
 
     dp = lax.axis_index("dp")
     y = lax.div(dp, 4)
@@ -131,6 +134,11 @@
 
     started = []
 
+    def flush(count):
+        for copy in started[:count]:
+            copy.wait_send()
+        del started[:count]
+
     def send(src, dst, snd, rcv, where):
         copy = pltpu.make_async_remote_copy(
             src_ref=src, dst_ref=dst, send_sem=snd, recv_sem=rcv, device_id=where, device_id_type=MESH
@@ -141,8 +149,10 @@
 
     get_w_in = pltpu.make_async_copy(w_in_hbm.at[:, pl.ds(pl.multiple_of(c * half, half), half)], w_in, w_sem.at[0])
     get_w_out = pltpu.make_async_copy(w_out_hbm.at[pl.ds(pl.multiple_of(c * half, half), half), :], w_out, w_sem.at[1])
-    get_w_out.start()
-    get_w_in.start()
+
+    get_frames = pltpu.make_async_copy(frames_hbm, frames_ref, w_sem.at[2])
+    get_up = pltpu.make_async_copy(up_hbm, up_ref, w_sem.at[3])
+    get_frames.start()
 
     barrier = pltpu.get_barrier_semaphore()
     greeted = 0
@@ -164,6 +174,10 @@
     sources += [partner]
     for where in sources:
         pl.semaphore_signal(barrier, inc=1, device_id=where, device_id_type=MESH)
+
+    get_up.start()
+    get_w_out.start()
+    get_w_in.start()
 
     nb = dest_ref.shape[1]
     nf = nb * run
@@ -189,10 +203,17 @@
         & (jnp.broadcast_to(mr, shape) < pair_rows)
     )
     place = jnp.where(hit, 1.0, 0.0)
-    msg[:, :width] = dot(place.astype(BF16), frames_ref[...]).astype(BF16)
     keep_row = keep_ref[...].reshape(1, nf).astype(F32)
     keep_col = jnp.sum(place * keep_row, axis=1, keepdims=True)
-    msg[:, width:] = jnp.broadcast_to(keep_col, (nm * ROWS16, LANE)).astype(BF16)
+    get_frames.wait()
+    packed = dot(place.astype(BF16), frames_ref[...])
+    flags = jnp.broadcast_to(keep_col, (nm * ROWS16, LANE))
+    lanes = width // LANE
+    spare = jnp.zeros((mrows - (lanes + 1) * pair_rows, LANE), F32)
+    for k in range(nm):
+        at = slice(k * ROWS16, k * ROWS16 + pair_rows)
+        parts = [packed[at, j * LANE : (j + 1) * LANE] for j in range(lanes)] + [flags[at, :], spare]
+        msg[pl.ds(k * mrows, mrows), :] = jnp.concatenate(parts, axis=0).astype(BF16)
     mine = pl.ds(pl.multiple_of(c * rows, rows), rows)
     theirs = pl.ds(pl.multiple_of(pc * rows, rows), rows)
 
@@ -202,8 +223,8 @@
 
     def a2a_send(k):
         g, dz, dc = kinds[k]
-        spot = pl.ds(pl.multiple_of((g * 4 + zh * 2 + c) * ROWS16, ROWS16), ROWS16)
-        part = msg.at[pl.ds(k * ROWS16, ROWS16), :]
+        spot = pl.ds(pl.multiple_of((g * 4 + zh * 2 + c) * mrows, ROWS16), mrows)
+        part = msg.at[pl.ds(k * mrows, mrows), :]
         copy = pltpu.make_async_remote_copy(
             src_ref=part,
             dst_ref=arr.at[spot, :],
@@ -237,28 +258,17 @@
     for k in range(4):
         locals_of[k] = a2a_send(k)
     local = locals_of[0]
+    get_up.wait()
     ups[mine, :] = (scale * up_ref[...].astype(F32)).astype(BF16)
     ucopy = send(ups.at[mine, :], ups.at[mine, :], u_snd.at[0], u_rcv.at[0], partner)
     get_w_out.wait()
     back_of(mine)
-    for k in range(4):
-        if k:
-            a2a[k].wait_send()
-        else:
-
-            @pl.when(x != 0)
-            def _():
-                a2a[0].wait_send()
-
     for k in range(4, nm):
         a2a_send(k)
     ucopy.wait_recv()
     back_of(theirs)
     get_w_in.wait()
 
-    ci, cj = iota((slab, 4 * ROWS16), 0), iota((slab, 4 * ROWS16), 1)
-    squeeze = (cj == lax.div(ci, pair_rows) * ROWS16 + lax.rem(ci, pair_rows)).astype(F32).astype(BF16)
-
     def rows_of(origin, g):
         ys = lax.rem(y - origin - NX * g + 2 * ny, ny)
         return tok.at[pl.ds(pl.multiple_of(c * rows + ys * slab, ROWS16), slab), :]
@@ -284,12 +294,14 @@
 
                 @pl.when(x != 0)
                 def _():
-                    a2a[0].wait_recv()
-            elif k < 4:
-                a2a[k].wait_recv()
+                    a2a[0].wait()
             else:
                 a2a[k].wait()
-        rows_of(x, g)[...] = dot(squeeze, arr[pl.ds(g * 4 * ROWS16, 4 * ROWS16), :]).astype(BF16)
+        got = arr[pl.ds(g * 4 * mrows, 4 * mrows), :].astype(F32)
+        mine_now = rows_of(x, g)
+        for j in range(lanes + 1):
+            parts = [got[m * mrows + j * pair_rows : m * mrows + (j + 1) * pair_rows, :] for m in range(4)]
+            mine_now[:, pl.ds(j * LANE, LANE)] = jnp.concatenate(parts, axis=0).astype(BF16)
         if g == 0:
             waits[3, g] = t_send(0, g, 0, 3, g, at_x(xn))
             waits[1, g] = t_send(0, g, 0, 1, 2 + g, at_x(xp))
@@ -445,6 +457,7 @@
     i_step(1, 6)
     i_step(0, 6)
 
+    gone = len(started)
     for q in range(IPARTS):
         ichain[0, q, zsteps].wait_recv()
         ichain[1, q, zsteps].wait_recv()
@@ -490,6 +503,7 @@
         for slot in range(NC * per_core):
             pltpu.make_async_copy(pce.at[t], fin.at[t, slot], f_rcv.at[t, slot]).wait()
 
+    flush(gone)
     for q in zcopies:
         q.wait_recv()
     sum_out = s_out[zh, pl.ds(start_of(zl), piece), :].astype(F32)
@@ -512,6 +526,7 @@
         part = enc_ref.at[xrows, :]
         ecopies.append(send(part, part, e_snd.at[d - 1], e_rcv.at[d - 1], at_x(wrap(x + d, NX))))
 
+    flush(len(started) - (nzl - 1))
     for q in ycopies:
         q.wait_recv()
     sum_in = s_in[y].astype(F32)
@@ -569,13 +584,14 @@
     nz = NZH * nzl
     ygroup = ny // NX
     nm = ygroup * 4
+    mrows = -(-(width // LANE + 1) * cap * run // ROWS16) * ROWS16
     grad_scale = float(nf * ny * 4 * nzl) ** (-0.5)
     quarter = rows // NX
     ysteps, zsteps = ny // 2, nz // 2
     core_rows = own_rows // NC
     dma = pltpu.SemaphoreType.DMA
     vm = pltpu.VMEM
-    pairs = [2, nm, 1, 16, 2 * OPARTS * ysteps, 2 * IPARTS * zsteps, nz - 1, ny - 1, (2, nzl), 1, NX - 1, NX - 1]
+    pairs = [4, nm, 1, 16, 2 * OPARTS * ysteps, 2 * IPARTS * zsteps, nz - 1, ny - 1, (2, nzl), 1, NX - 1, NX - 1]
     sems = []
     for i, n in enumerate(pairs):
         shape = n if isinstance(n, tuple) else (n,)
@@ -589,13 +605,15 @@
             jax.ShapeDtypeStruct((core_rows, units), F32),
             jax.ShapeDtypeStruct((core_rows, units), F32),
         ),
-        in_specs=[vspec, vspec, vspec, vspec, vspec, aspec, aspec, vspec],
+        in_specs=[vspec, vspec, aspec, vspec, vspec, aspec, aspec, aspec],
         out_specs=(vspec, vspec, vspec),
         scratch_shapes=[
             vm((width, half), BF16),
             vm((half, width), BF16),
-            vm((nm * ROWS16, width + LANE), BF16),
-            vm((nm * ROWS16, width + LANE), BF16),
+            vm((nf, width), BF16),
+            vm((rows, width), BF16),
+            vm((nm * mrows, LANE), BF16),
+            vm((nm * mrows, LANE), BF16),
             vm((NC * rows, width + LANE), BF16),
             vm((NC * rows, width), BF16),
             vm((width, NC * rows), BF16),

time: 93.2 us -> 90.3 us (0.969)
  Pallas kernels: 92.4 us -> 89.5 us
    pallas_call x1, Pallas kernels: 90.2 us -> 87.3 us  [shards(): pl.pallas_call(functools.partial(kernel, (ny, nzl, cap, run, 0.5 * grad_s...]
where the time goes in v3:
time: 90.3 us; the launch traced here: 90.1 us
  Pallas kernels  89.5 us (99%)
    pallas_call x1, Pallas kernels, shards(): pl.pallas_call(functools.partial(kernel, (ny, nzl, cap, run, 0.5 * grad_s...  87.3 us
    pallas_call x1, Pallas kernels, shards(): pl.pallas_call(place_outputs, out_shape=tuple((jax.ShapeDtypeStruct(v.sha...  2.2 us

profile of v3, /device:TPU:1, one launch (start us, length us, event | category | flops | bytes accessed | tf_op | source)
XLA Modules:
  0.0 90.1 jit_solution(10690514365151388324)
XLA Ops:
  0.6 87.3 %ffn_step.1 = (bf16[384,1024]{1,0:T(8,128)(2,1)}, f32[32,1024]{1,0:T(8,128)}, f32[32,1024]{1,0:T(8,128)}) custom-call(s32[1,72]{1,0:T(1,128)} %bitcast.6, s32[288]{0:T(512)} %keep_ref.1, bf16[288,1024]{1,0:T(8,128)(2,1)} %frames_hbm.1, f32[1,1024]{1,0:T(1,128)} %bitcast.4, f32[1,1024]{1,0:T(1,128)} %bitcast.5, bf16[1024,1024]{1,0:T(8,128)(2,1)} %w_in_hbm.1, ...), custom_call_target="tpu_custom_call" | custom-call | tf_op jit(solution)/shard_map/ffn_step/pallas_call | solution.py:601
  87.9 2.2 %place_outputs.1 = (bf16[384,1024]{1,0:T(8,128)(2,1)}, f32[32,1024]{1,0:T(8,128)}, f32[32,1024]{1,0:T(8,128)}) custom-call(bf16[384,1024]{1,0:T(8,128)(2,1)} %get-tuple-element.9.enc, f32[32,1024]{1,0:T(8,128)} %get-tuple-element.10.gin, f32[32,1024]{1,0:T(8,128)} %get-tuple-element.11.gout), custom_call_target="tpu_custom_call" | custom-call | tf_op jit(solution)/shard_map/place_outputs/pallas_call | solution.py:655

commit v4 on v3

--- a/solution.py
+++ b/solution.py
@@ -322,13 +322,10 @@
     for g in range(ygroup):
         waits[2, g].wait_recv()
         waits["c", 2, g] = t_send(2, g, 1, 2, 12 + g, partner)
-    for o in (0, 3, 1, 2):
-        for g in range(ygroup):
-            waits["c", o, g].wait_recv()
-
     step_rows = LANE
-    for t in range(2 * rows // step_rows):
-        at = pl.ds(t * step_rows, step_rows)
+
+    def forward(begin):
+        at = pl.ds(pl.multiple_of(begin, step_rows), step_rows)
         feat = tok[at, :width].astype(F32)
         live = tok[at, width:][:, 0:1].astype(F32)
         mean = jnp.mean(feat, axis=1, keepdims=True)
@@ -340,6 +337,14 @@
         sig = jax.nn.sigmoid(pre)
         hid[at, :] = (live * (pre * sig)).astype(BF16)
         act[at, :] = (live * back[at, :] * (sig + pre * sig * (1.0 - sig))).astype(BF16)
+
+    for t in range(rows // step_rows):
+        forward(c * rows + t * step_rows)
+    for o in (0, 3, 1, 2):
+        for g in range(ygroup):
+            waits["c", o, g].wait_recv()
+    for t in range(rows // step_rows):
+        forward(pc * rows + t * step_rows)
 
     def gradient(left, right, out):
         block = 2 * LANE

time: 90.3 us -> 87.6 us (0.970)
  Pallas kernels: 89.5 us -> 86.7 us
    pallas_call x1, Pallas kernels: 87.3 us -> 84.5 us  [shards(): pl.pallas_call(functools.partial(kernel, (ny, nzl, cap, run, 0.5 * grad_s...]
where the time goes in v4:
time: 87.6 us; the launch traced here: 87.3 us
  Pallas kernels  86.7 us (99%)
    pallas_call x1, Pallas kernels, shards(): pl.pallas_call(functools.partial(kernel, (ny, nzl, cap, run, 0.5 * grad_s...  84.5 us
    pallas_call x1, Pallas kernels, shards(): pl.pallas_call(place_outputs, out_shape=tuple((jax.ShapeDtypeStruct(v.sha...  2.2 us

profile of v4, /device:TPU:1, one launch (start us, length us, event | category | flops | bytes accessed | tf_op | source)
XLA Modules:
  0.0 87.3 jit_solution(7175305373838913069)
XLA Ops:
  0.6 84.5 %ffn_step.1 = (bf16[384,1024]{1,0:T(8,128)(2,1)}, f32[32,1024]{1,0:T(8,128)}, f32[32,1024]{1,0:T(8,128)}) custom-call(s32[1,72]{1,0:T(1,128)} %bitcast.6, s32[288]{0:T(512)} %keep_ref.1, bf16[288,1024]{1,0:T(8,128)(2,1)} %frames_hbm.1, f32[1,1024]{1,0:T(1,128)} %bitcast.4, f32[1,1024]{1,0:T(1,128)} %bitcast.5, bf16[1024,1024]{1,0:T(8,128)(2,1)} %w_in_hbm.1, ...), custom_call_target="tpu_custom_call" | custom-call | tf_op jit(solution)/shard_map/ffn_step/pallas_call | solution.py:606
  85.1 2.2 %place_outputs.1 = (bf16[384,1024]{1,0:T(8,128)(2,1)}, f32[32,1024]{1,0:T(8,128)}, f32[32,1024]{1,0:T(8,128)}) custom-call(bf16[384,1024]{1,0:T(8,128)(2,1)} %get-tuple-element.9.enc, f32[32,1024]{1,0:T(8,128)} %get-tuple-element.10.gin, f32[32,1024]{1,0:T(8,128)} %get-tuple-element.11.gout), custom_call_target="tpu_custom_call" | custom-call | tf_op jit(solution)/shard_map/place_outputs/pallas_call | solution.py:660

commit v5 on v4

--- a/solution.py
+++ b/solution.py
@@ -219,7 +219,7 @@
 
     pl.semaphore_wait(barrier, len(sources))
 
-    a2a = []
+    a2a = {}
 
     def a2a_send(k):
         g, dz, dc = kinds[k]
@@ -233,7 +233,7 @@
             device_id=a2a_id(lax.rem(y + x + NX * g, ny), dz, dc),
             device_id_type=MESH,
         )
-        a2a.append(copy)
+        a2a[k] = copy
         if k:
             copy.start()
             return None
@@ -255,7 +255,7 @@
         ups_t[:, where] = u.T
 
     locals_of = {}
-    for k in range(4):
+    for k in (2, 3, 6, 7, 0, 1, 4, 5):
         locals_of[k] = a2a_send(k)
     local = locals_of[0]
     get_up.wait()
@@ -263,8 +263,6 @@
     ucopy = send(ups.at[mine, :], ups.at[mine, :], u_snd.at[0], u_rcv.at[0], partner)
     get_w_out.wait()
     back_of(mine)
-    for k in range(4, nm):
-        a2a_send(k)
     ucopy.wait_recv()
     back_of(theirs)
     get_w_in.wait()
@@ -432,8 +430,6 @@
     o_step(1, 3)
     i_step(0, 3)
     o_step(0, 3)
-    i_step(1, 4)
-    o_step(1, 4)
     pcopy.wait_recv()
     q_sum[...] = (p_own[...] + p_rcv[...].astype(F32)).astype(BF16)
     qcopies = []
@@ -441,6 +437,8 @@
         to = wrap(x + d, NX)
         part = q_sum.at[pl.ds(pl.multiple_of(to * quarter, quarter), quarter), :]
         qcopies.append(send(part, q_rcv.at[d - 1], q_snd.at[d - 1], q_rsm.at[d - 1], at_x(to)))
+    i_step(1, 4)
+    o_step(1, 4)
     i_step(0, 4)
     o_step(0, 4)
     i_step(1, 5)

time: 87.6 us -> 87.4 us (level)
  no operation moved by 1% of the time
where the time goes in v5:
time: 87.4 us; the launch traced here: 87.2 us
  Pallas kernels  86.6 us (99%)
    pallas_call x1, Pallas kernels, shards(): pl.pallas_call(functools.partial(kernel, (ny, nzl, cap, run, 0.5 * grad_s...  84.4 us
    pallas_call x1, Pallas kernels, shards(): pl.pallas_call(place_outputs, out_shape=tuple((jax.ShapeDtypeStruct(v.sha...  2.2 us

profile of v5, /device:TPU:1, one launch (start us, length us, event | category | flops | bytes accessed | tf_op | source)
XLA Modules:
  0.0 87.2 jit_solution(862478752581220266)
XLA Ops:
  0.6 84.4 %ffn_step.1 = (bf16[384,1024]{1,0:T(8,128)(2,1)}, f32[32,1024]{1,0:T(8,128)}, f32[32,1024]{1,0:T(8,128)}) custom-call(s32[1,72]{1,0:T(1,128)} %bitcast.6, s32[288]{0:T(512)} %keep_ref.1, bf16[288,1024]{1,0:T(8,128)(2,1)} %frames_hbm.1, f32[1,1024]{1,0:T(1,128)} %bitcast.4, f32[1,1024]{1,0:T(1,128)} %bitcast.5, bf16[1024,1024]{1,0:T(8,128)(2,1)} %w_in_hbm.1, ...), custom_call_target="tpu_custom_call" | custom-call | tf_op jit(solution)/shard_map/ffn_step/pallas_call | solution.py:604
  85.0 2.2 %place_outputs.1 = (bf16[384,1024]{1,0:T(8,128)(2,1)}, f32[32,1024]{1,0:T(8,128)}, f32[32,1024]{1,0:T(8,128)}) custom-call(bf16[384,1024]{1,0:T(8,128)(2,1)} %get-tuple-element.9.enc, f32[32,1024]{1,0:T(8,128)} %get-tuple-element.10.gin, f32[32,1024]{1,0:T(8,128)} %get-tuple-element.11.gout), custom_call_target="tpu_custom_call" | custom-call | tf_op jit(solution)/shard_map/place_outputs/pallas_call | solution.py:658
